TPU v7x, 32 devices: a whole 2x2x4 slice. The times are simulated.
32 devices in a mesh: dp: 2 (over core), expert: 16 (over z, y, x).
Axes of the slice: x: 2, y: 2, z: 4, core: 2. Of those that a mesh axis runs over, the one named last changes fastest.
Arguments:
- tokens_in: bfloat16 [4096, 2048], P(('dp', 'expert')), may hold values from -6 to 6
- grad_out: bfloat16 [4096, 2048], P(('dp', 'expert')), may hold values from -6 to 6
- routes: int32 [4096, 8], P(('dp', 'expert')), may hold values from 0 to 15, all different within a row; in each aligned block of 128 rows (0 to 127, 128 to 255, ...) at most 66 rows name the same one
- router_weight: bfloat16 [2048, 16], replicated, may hold values from -0.125 to 0.125
- w_gate: bfloat16 [16, 768, 2048], P('expert'), may hold values from -0.125 to 0.125
- w_up: bfloat16 [16, 768, 2048], P('expert'), may hold values from -0.125 to 0.125
- w_down: bfloat16 [16, 768, 2048], P('expert'), may hold values from -0.21875 to 0.21875
Outputs:
- grad_x: bfloat16 [4096, 2048], P(('dp', 'expert'))
- grad_gate: bfloat16 [16, 768, 2048], P('expert', 'dp')
- grad_up: bfloat16 [16, 768, 2048], P('expert', 'dp')
- grad_down: bfloat16 [16, 768, 2048], P('expert', 'dp')
- grad_router: float32 [2048, 16], replicated
Inputs may be any that keep to these rules, and one draw needn't show every extreme that they name: `routes`: each row names 8 different experts. Among the 128 rows of one device no expert is named more than 66 times, and in every draw some expert is named exactly 66 times by the rows of some device.
All inputs are finite; a program needn't handle non-finite values.
Results may differ from a plain program's by a relative error of at most 0.009.
Values may be sent and summed in bfloat16 or wider, within the bound.
No kernel may reach another device: no remote copies, remote signals or barrier semaphores. Data moves between devices by JAX's collectives and lax.ppermute only.
A program may use at most 192 MiB of HBM per device.

v0:
```python
import jax
import jax.numpy as jnp
from jax import lax
from jax.sharding import PartitionSpec as P


def local(tokens_in, grad_out, routes, router_weight, w_gate, w_up, w_down):
    tok_count = tokens_in.shape[0]
    width = tokens_in.shape[1]
    top_count = routes.shape[1]
    expert_count = router_weight.shape[1]
    capacity = tok_count * top_count // expert_count + 2
    pairs = tok_count * top_count
    logits = jnp.dot(tokens_in, router_weight, preferred_element_type=jnp.float32)
    chosen = jnp.take_along_axis(logits, routes, axis=1)
    probs = jax.nn.softmax(chosen, axis=1)
    flat_routes = routes.reshape(-1)
    columns = jnp.arange(expert_count, dtype=jnp.int32)
    onehot = (flat_routes[:, None] == columns[None, :]).astype(jnp.int32)
    rank = jnp.sum((jnp.cumsum(onehot, axis=0) - 1) * onehot, axis=1)
    slot = flat_routes * capacity + rank
    source = (
        jnp.full((expert_count * capacity,), pairs, jnp.int32)
        .at[slot]
        .set(jnp.arange(pairs, dtype=jnp.int32))
    )
    live = source < pairs
    safe_source = jnp.minimum(source, pairs - 1)
    source_tok = safe_source // top_count
    sent_x = jnp.where(live[:, None], tokens_in[source_tok], jnp.zeros((), jnp.bfloat16))
    gate_prob = jnp.where(live, probs.reshape(-1)[safe_source], jnp.float32(0.0))
    sent_s = (gate_prob[:, None] * grad_out[source_tok].astype(jnp.float32)).astype(jnp.bfloat16)
    sent_x = sent_x.reshape(expert_count, capacity, width)
    sent_s = sent_s.reshape(expert_count, capacity, width)
    recv_x, recv_s = (
        lax.all_to_all(sent_x, "expert", split_axis=0, concat_axis=0, tiled=True),
        lax.all_to_all(sent_s, "expert", split_axis=0, concat_axis=0, tiled=True),
    )
    senders = recv_x.shape[0]
    rows_x = recv_x.reshape(senders * capacity, width)
    rows_s = recv_s.reshape(senders * capacity, width)
    gate_w = w_gate[0]
    up_w = w_up[0]
    down_w = w_down[0]
    pre_gate = jnp.einsum("rd,fd->rf", rows_x, gate_w, preferred_element_type=jnp.float32)
    pre_up = jnp.einsum("rd,fd->rf", rows_x, up_w, preferred_element_type=jnp.float32)
    sig = jax.nn.sigmoid(pre_gate)
    act = pre_gate * sig
    hidden = (act * pre_up).astype(jnp.bfloat16)
    grad_hidden = jnp.einsum("rd,fd->rf", rows_s, down_w, preferred_element_type=jnp.float32)
    weighted = jnp.sum(hidden.astype(jnp.float32) * grad_hidden, axis=1)
    back_scores = lax.all_to_all(
        weighted.reshape(senders, capacity), "expert", split_axis=0, concat_axis=0, tiled=True
    )
    grad_pg = (grad_hidden * pre_up * sig * (1.0 + pre_gate * (1.0 - sig))).astype(jnp.bfloat16)
    grad_pu = (grad_hidden * act).astype(jnp.bfloat16)
    part = (
        jnp.dot(grad_pg, gate_w, preferred_element_type=jnp.float32)
        + jnp.dot(grad_pu, up_w, preferred_element_type=jnp.float32)
    ).astype(jnp.bfloat16)
    back_parts = lax.all_to_all(
        part.reshape(senders, capacity, width), "expert", split_axis=0, concat_axis=0, tiled=True
    )
    pair_scores = back_scores.reshape(-1)[slot].reshape(tok_count, top_count)
    dchosen = pair_scores - probs * jnp.sum(pair_scores, axis=1, keepdims=True)
    dlogits = jnp.sum(
        dchosen[:, :, None] * (routes[:, :, None] == columns[None, None, :]).astype(jnp.float32),
        axis=1,
    ).astype(jnp.bfloat16)
    router_term = jnp.dot(tokens_in.T, dlogits, preferred_element_type=jnp.float32)
    grad_router = lax.psum(router_term, ("dp", "expert")) / tok_count
    pair_parts = back_parts.reshape(expert_count * capacity, width)[slot].reshape(
        tok_count, top_count, width
    )
    part_sum = jnp.sum(pair_parts.astype(jnp.float32), axis=1)
    grad_x = (
        part_sum + jnp.dot(dlogits, router_weight.T, preferred_element_type=jnp.float32)
    ).astype(jnp.bfloat16)
    term_gate = jnp.einsum("rf,rd->fd", grad_pg, rows_x, preferred_element_type=jnp.float32)
    term_up = jnp.einsum("rf,rd->fd", grad_pu, rows_x, preferred_element_type=jnp.float32)
    term_down = jnp.einsum("rf,rd->fd", hidden, rows_s, preferred_element_type=jnp.float32)
    summed = lax.psum_scatter(
        jnp.concatenate([term_gate, term_up, term_down], axis=1).astype(jnp.bfloat16),
        "dp",
        scatter_dimension=0,
        tiled=True,
    ).astype(jnp.float32)
    grad_gate = summed[:, :width].astype(jnp.bfloat16)[None]
    grad_up = summed[:, width : 2 * width].astype(jnp.bfloat16)[None]
    grad_down = summed[:, 2 * width :].astype(jnp.bfloat16)[None]
    return (grad_x, grad_gate, grad_up, grad_down, grad_router)


def solution(mesh):
    return jax.shard_map(
        local,
        mesh=mesh,
        in_specs=(
            P(("dp", "expert"), None),
            P(("dp", "expert"), None),
            P(("dp", "expert"), None),
            P(),
            P("expert", None, None),
            P("expert", None, None),
            P("expert", None, None),
        ),
        out_specs=(
            P(("dp", "expert"), None),
            P("expert", "dp", None),
            P("expert", "dp", None),
            P("expert", "dp", None),
            P(),
        ),
        check_vma=False,
    )
```

profile of v0, /device:TPU:0, one launch (start us, length us, event | category | flops | bytes accessed | tf_op | source)
XLA Modules:
  0.0 535.3 jit_solution(11170974910179655234)
XLA Ops:
  10.5 4.5 reduce-window.6
  21.5 7.0 %gather_fusion.5 = f32[1024]{0:T(1024)S(1)} fusion(f32[128,16]{0,1:T(8,128)S(1)} %fusion.24, s32[1024]{0:T(1024)S(1)} %reshape.202), kind=kCustom, calls=%fused_computation.5 | custom fusion | bytes 16384 | tf_op jit(solution)/shard_map/jit(take_along_axis)/gather | solution.py:15
  33.5 11.6 %gather_fusion.2 = bf16[1056,2048]{1,0:T(8,128)(2,1)} fusion(bf16[128,2048]{1,0:T(8,128)(2,1)} %param.7, s32[2048]{0:T(1024)S(1)} %get-tuple-element.16), kind=kCustom, calls=%fused_computation.2 | custom fusion | bytes 8654976 | tf_op jit(solution)/shard_map/gather | solution.py:30
  45.1 5.3 gather.25
  50.4 4.9 broadcast_select_fusion
  55.3 8.4 %all-to-all-start.1 = ((bf16[16,66,2048]{2,1,0:T(8,128)(2,1)}), bf16[16,66,2048]{2,1,0:T(8,128)(2,1)}, u32[]{:S(2)}, u32[]{:S(2)}) async-start(bf16[16,66,2048]{2,1,0:T(8,128)(2,1)} %broadcast_select_fusion), calls=%async_computation.1 | async-start | bytes 9437184 | tf_op jit(solution)/shard_map/all_to_all | solution.py:36
  63.7 11.6 %gather_fusion.1 = bf16[1056,2048]{1,0:T(8,128)(2,1)} fusion(bf16[128,2048]{1,0:T(8,128)(2,1)} %param.8, s32[2048]{0:T(1024)S(1)} %get-tuple-element.16), kind=kCustom, calls=%fused_computation.1 | custom fusion | bytes 8654976 | tf_op jit(solution)/shard_map/gather | solution.py:32
  75.4 6.6 %reshape.160 = f32[16,66,2048]{2,1,0:T(8,128)} reshape(bf16[1056,2048]{1,0:T(8,128)(2,1)} %gather_fusion.1) | data formatting | bytes 12976128 | tf_op jit(solution)/shard_map/convert_element_type | solution.py:32
  81.9 6.5 %multiply_convert_fusion = bf16[16,66,2048]{2,1,0:T(8,128)(2,1)} fusion(f32[16,66,2048]{2,1,0:T(8,128)} %reshape.160, f32[16,66]{1,0:T(8,128)S(1)} %mul.76), kind=kLoop, calls=%fused_computation.8 | loop fusion | flops 4325376 | bytes 12980352 | tf_op jit(solution)/shard_map/convert_element_type | solution.py:32
  88.4 64.5 %all-to-all-done.1 = bf16[16,66,2048]{2,1,0:T(8,128)(2,1)} async-done(((bf16[16,66,2048]{2,1,0:T(8,128)(2,1)}), bf16[16,66,2048]{2,1,0:T(8,128)(2,1)}, u32[]{:S(2)}, u32[]{:S(2)}) %all-to-all-start.1) | async-done | bytes 4325408 | tf_op jit(solution)/shard_map/all_to_all | solution.py:36
  152.9 22.6 %all-to-all-start = ((bf16[16,66,2048]{2,1,0:T(8,128)(2,1)}), bf16[16,66,2048]{2,1,0:T(8,128)(2,1)}, u32[]{:S(2)}, u32[]{:S(2)}) async-start(bf16[16,66,2048]{2,1,0:T(8,128)(2,1)} %multiply_convert_fusion), calls=%async_computation | async-start | bytes 9437184 | tf_op jit(solution)/shard_map/all_to_all | solution.py:37
  175.5 5.3 reshape.155
  180.8 7.6 %fusion.4 = f32[1056,768]{1,0:T(8,128)} fusion(bf16[1056,2048]{1,0:T(8,128)(2,1)} %reshape.155, bf16[1,768,2048]{2,1,0:T(8,128)(2,1)S(1)} %copy-done), kind=kOutput, calls=%fused_computation.24 | convolution fusion | flops 3321888768 | bytes 10715136 | tf_op jit(solution)/shard_map/rd,fd->rf/dot_general | solution.py:45
  188.5 5.3 fusion.7
  193.7 69.3 %all-to-all-done = bf16[16,66,2048]{2,1,0:T(8,128)(2,1)} async-done(((bf16[16,66,2048]{2,1,0:T(8,128)(2,1)}), bf16[16,66,2048]{2,1,0:T(8,128)(2,1)}, u32[]{:S(2)}, u32[]{:S(2)}) %all-to-all-start) | async-done | bytes 4325408 | tf_op jit(solution)/shard_map/all_to_all | solution.py:37
  263.1 5.4 %reshape.154 = bf16[1056,2048]{1,0:T(8,128)(2,1)} reshape(bf16[16,66,2048]{2,1,0:T(8,128)(2,1)} %all-to-all-done) | data formatting | bytes 8650752 | tf_op jit(solution)/shard_map/reshape | solution.py:41
  268.5 10.9 %multiply_reduce_fusion = (f32[1056]{0:T(1024)S(1)}, bf16[1056,768]{1,0:T(8,128)(2,1)S(1)}, bf16[1056,768]{1,0:T(8,128)(2,1)}, bf16[1056,768]{1,0:T(8,128)(2,1)S(1)}) fusion(f32[1056,768]{1,0:T(8,128)} %fusion.7, f32[1056,768]{1,0:T(8,128)} %fusion.4, bf16[1056,2048]{1,0:T(8,128)(2,1)} %reshape.154, bf16[1,768,2048]{2,1,0:T(8,128)(2,1)} %param.13), kind=kOutput, calls=%fused_computation.16 | convolution fusion | flops 3336485888 | bytes 18829440 | tf_op jit(solution)/shard_map/rd,fd->rf/dot_general | solution.py:50
  279.3 5.9 %convolution_convert_fusion = bf16[768,2048]{1,0:T(8,128)(2,1)} fusion(bf16[1056,768]{1,0:T(8,128)(2,1)S(1)} %get-tuple-element.6, bf16[1056,2048]{1,0:T(8,128)(2,1)S(1)} %copy-done.2), kind=kOutput, calls=%fused_computation.13 | convolution fusion | flops 3323461632 | bytes 9093120 | tf_op jit(solution)/shard_map/rf,rd->fd/dot_general | solution.py:81
  285.2 5.7 %convolution_convert_fusion.1 = bf16[768,2048]{1,0:T(8,128)(2,1)} fusion(bf16[1056,768]{1,0:T(8,128)(2,1)S(1)} %get-tuple-element.10, bf16[1056,2048]{1,0:T(8,128)(2,1)S(1)} %bitcast.64), kind=kOutput, calls=%fused_computation.14 | convolution fusion | flops 3323461632 | bytes 9093120 | tf_op jit(solution)/shard_map/rf,rd->fd/dot_general | solution.py:80
  291.6 21.7 %all-to-all-start.3 = ((f32[16,1,66]{2,1,0:T(1,128)}), f32[16,1,66]{2,1,0:T(1,128)S(1)}, u32[]{:S(2)}, u32[]{:S(2)}) async-start(f32[16,1,66]{2,1,0:T(1,128)} %all_to_all.18), calls=%async_computation.3 | async-start | bytes 16384 | tf_op jit(solution)/shard_map/all_to_all | solution.py:52
  313.3 8.7 %convolution_convert_fusion.2 = bf16[768,2048]{1,0:T(8,128)(2,1)} fusion(bf16[1056,768]{1,0:T(8,128)(2,1)} %get-tuple-element.9, bf16[1056,2048]{1,0:T(8,128)(2,1)} %reshape.155), kind=kOutput, calls=%fused_computation.15 | convolution fusion | flops 3323461632 | bytes 9093120 | tf_op jit(solution)/shard_map/rf,rd->fd/dot_general | solution.py:79
  323.3 6.2 %gather_fusion.4 = f32[1024]{0:T(1024)S(1)} fusion(f32[1056]{0:T(1024)S(1)} %reshape.158, s32[1024]{0:T(1024)S(1)} %broadcast_clamp_fusion), kind=kCustom, calls=%fused_computation.4 | custom fusion | bytes 12288 | tf_op jit(solution)/shard_map/gather | solution.py:64
  331.7 9.5 %pad_maximum_fusion = bf16[768,6144]{1,0:T(8,128)(2,1)} fusion(bf16[768,2048]{1,0:T(8,128)(2,1)} %convolution_convert_fusion, bf16[768,2048]{1,0:T(8,128)(2,1)} %convolution_convert_fusion.1, bf16[768,2048]{1,0:T(8,128)(2,1)} %convolution_convert_fusion.2), kind=kLoop, calls=%fused_computation.7 | loop fusion | flops 28311552 | bytes 18874368 | tf_op jit(solution)/shard_map/concatenate | solution.py:83
  341.3 5.1 fusion.2
  346.5 5.2 fusion
  351.7 6.1 %reshape.156 = bf16[16,66,2048]{2,1,0:T(8,128)(2,1)} reshape(bf16[1056,2048]{1,0:T(8,128)(2,1)} %fusion) | data formatting | bytes 8650752 | tf_op jit(solution)/shard_map/reshape | solution.py:62
  357.7 6.9 %all-to-all-start.2 = ((bf16[16,66,2048]{2,1,0:T(8,128)(2,1)}), bf16[16,66,2048]{2,1,0:T(8,128)(2,1)}, u32[]{:S(2)}, u32[]{:S(2)}) async-start(bf16[16,66,2048]{2,1,0:T(8,128)(2,1)} %reshape.156), calls=%async_computation.2 | async-start | bytes 9437184 | tf_op jit(solution)/shard_map/all_to_all | solution.py:61
  364.6 133.3 %all-reduce.2.cloned.1.call-done = f32[2048,16]{0,1:T(8,128)} async-done(((f32[2048,16]{0,1:T(8,128)}), f32[2048,16]{0,1:T(8,128)}) %all-reduce.2.cloned.1.call-update) | async-done | bytes 131088 | tf_op jit(solution)/shard_map/psum | solution.py:71
  499.5 5.4 %reshape.157 = bf16[1056,2048]{1,0:T(8,128)(2,1)} reshape(bf16[16,66,2048]{2,1,0:T(8,128)(2,1)} %all-to-all-done.2) | data formatting | bytes 8650752 | tf_op jit(solution)/shard_map/reshape | solution.py:72
  504.9 11.6 %gather_fusion.3 = bf16[1024,2048]{1,0:T(8,128)(2,1)} fusion(bf16[1056,2048]{1,0:T(8,128)(2,1)} %reshape.157, s32[1024]{0:T(1024)S(1)} %broadcast_clamp_fusion), kind=kCustom, calls=%fused_computation.3 | custom fusion | bytes 8392704 | tf_op jit(solution)/shard_map/gather | solution.py:72
  516.6 5.1 convert_reduce_fusion
  522.7 4.7 slice_bitcast_fusion
  (77 shorter events, 20.9 us)
Async XLA Ops:
  8.0 172.8 %copy-start = (bf16[1,768,2048]{2,1,0:T(8,128)(2,1)S(1)}, bf16[1,768,2048]{2,1,0:T(8,128)(2,1)}, u32[]{:S(2)}) copy-start(bf16[1,768,2048]{2,1,0:T(8,128)(2,1)} %param.11) | copy-start | bytes 9437188
  21.5 7.2 %copy-start.4 = (s32[128,8]{0,1:T(8,128)S(1)}, s32[128,8]{0,1:T(8,128)}, u32[]{:S(2)}) copy-start(s32[128,8]{0,1:T(8,128)} %param.9) | copy-start | bytes 12292
  55.3 97.6 %all-to-all-start.1 = ((bf16[16,66,2048]{2,1,0:T(8,128)(2,1)}), bf16[16,66,2048]{2,1,0:T(8,128)(2,1)}, u32[]{:S(2)}, u32[]{:S(2)}) async-start(bf16[16,66,2048]{2,1,0:T(8,128)(2,1)} %broadcast_select_fusion), calls=%async_computation.1 | async-start | bytes 9437184 | tf_op jit(solution)/shard_map/all_to_all | solution.py:36
  152.9 110.1 %all-to-all-start = ((bf16[16,66,2048]{2,1,0:T(8,128)(2,1)}), bf16[16,66,2048]{2,1,0:T(8,128)(2,1)}, u32[]{:S(2)}, u32[]{:S(2)}) async-start(bf16[16,66,2048]{2,1,0:T(8,128)(2,1)} %multiply_convert_fusion), calls=%async_computation | async-start | bytes 9437184 | tf_op jit(solution)/shard_map/all_to_all | solution.py:37
  180.8 7.6 %copy-start.1 = (bf16[1056,2048]{1,0:T(8,128)(2,1)S(1)}, bf16[1056,2048]{1,0:T(8,128)(2,1)}, u32[]{:S(2)}) copy-start(bf16[1056,2048]{1,0:T(8,128)(2,1)} %reshape.155) | copy-start | bytes 12976132
  180.8 7.6 %copy-start.5 = (bf16[1,768,2048]{2,1,0:T(8,128)(2,1)S(1)}, bf16[1,768,2048]{2,1,0:T(8,128)(2,1)}, u32[]{:S(2)}) copy-start(bf16[1,768,2048]{2,1,0:T(8,128)(2,1)} %param.12) | copy-start | bytes 9437188
  263.1 22.1 %slice-start = ((s8[4325376]{0:T(1024)(128)(4,1)}), s8[131072]{0:T(1024)(128)(4,1)S(1)}, s32[]{:S(2)}) async-start(s8[4325376]{0:T(1024)(128)(4,1)} %bitcast.63), calls=%async_computation.7 | async-start | bytes 262144
  268.5 10.9 %copy-start.2 = (bf16[1056,2048]{1,0:T(8,128)(2,1)S(1)}, bf16[1056,2048]{1,0:T(8,128)(2,1)}, u32[]{:S(2)}) copy-start(bf16[1056,2048]{1,0:T(8,128)(2,1)} %reshape.154) | copy-start | bytes 12976132
  268.5 16.7 %slice-start.1 = ((s8[4325376]{0:T(1024)(128)(4,1)}), s8[4194304]{0:T(1024)(128)(4,1)S(1)}, s32[]{:S(2)}) async-start(s8[4325376]{0:T(1024)(128)(4,1)} %bitcast.63), calls=%async_computation.8 | async-start | bytes 8388608
  279.3 5.9 %copy-start.7 = (bf16[1056,768]{1,0:T(8,128)(2,1)}, bf16[1056,768]{1,0:T(8,128)(2,1)S(1)}, u32[]{:S(2)}) copy-start(bf16[1056,768]{1,0:T(8,128)(2,1)S(1)} %get-tuple-element.10) | copy-start | bytes 4866052
  291.6 30.4 %all-to-all-start.3 = ((f32[16,1,66]{2,1,0:T(1,128)}), f32[16,1,66]{2,1,0:T(1,128)S(1)}, u32[]{:S(2)}, u32[]{:S(2)}) async-start(f32[16,1,66]{2,1,0:T(1,128)} %all_to_all.18), calls=%async_computation.3 | async-start | bytes 16384 | tf_op jit(solution)/shard_map/all_to_all | solution.py:52
  313.3 184.7 %all-reduce.2.cloned.1.call-start = ((), (), s32[]{:S(2)}) async-start(), calls=%async_computation.6 | async-start | bytes 262144 | tf_op jit(solution)/shard_map/psum | solution.py:71
  331.7 191.0 %reduce-scatter.2.cloned.1.call-start = ((), (), s32[]{:S(2)}) async-start(), calls=%async_computation.5 | async-start | bytes 14155776 | tf_op jit(solution)/shard_map/reduce_scatter | solution.py:82
  341.3 5.1 copy-start.6
  341.3 5.1 copy-start.8
  357.7 141.8 %all-to-all-start.2 = ((bf16[16,66,2048]{2,1,0:T(8,128)(2,1)}), bf16[16,66,2048]{2,1,0:T(8,128)(2,1)}, u32[]{:S(2)}, u32[]{:S(2)}) async-start(bf16[16,66,2048]{2,1,0:T(8,128)(2,1)} %reshape.156), calls=%async_computation.2 | async-start | bytes 9437184 | tf_op jit(solution)/shard_map/all_to_all | solution.py:61
  516.6 5.1 copy-start.3
Sparse Core Ops, SparseCore 0:
  331.8 166.0 all-reduce.1
Sparse Core Ops, SparseCore 1:
  341.4 18.9 reduce-scatter.1
where the time goes:
time: 543 us; the launch traced here: 535 us
  waiting for transfers between devices  267 us (49%)
  local copies, waits for them, and re-layouts  99.3 us (18%)
  starting transfers between devices  59.6 us (11%)
  matrix products  58.6 us (11%)
  other arithmetic  34.5 us (6%)
  between operations  16.2 us (3%)
    psum x1, waiting for transfers between devices, local(): grad_router = lax.psum(router_term, ('dp', 'expert')) / tok_count  133 us
    all_to_all x1, waiting for transfers between devices, local(): lax.all_to_all(sent_s, 'expert', split_axis=0, concat_axis=0, tiled=True)  69.3 us
    all_to_all x1, waiting for transfers between devices, local(): lax.all_to_all(sent_x, 'expert', split_axis=0, concat_axis=0, tiled=True)  64.5 us
    all_to_all x1, starting transfers between devices, local(): lax.all_to_all(sent_s, 'expert', split_axis=0, concat_axis=0, tiled=True)  22.6 us
    all_to_all x1, starting transfers between devices, local(): lax.all_to_all(weighted.reshape(senders, capacity), 'expert', split_axis=...  21.7 us
    gather x2, local copies, waits for them, and re-layouts, local(): tokens_in[source_tok]  16.9 us
    gather x1, local copies, waits for them, and re-layouts, local(): grad_out[source_tok].astype(jnp.float32)  11.6 us
    gather x1, local copies, waits for them, and re-layouts, local(): back_parts.reshape(expert_count * capacity, width)[slot]  11.6 us
  transfers between devices with their start and end apart: 6, of which 3 were waited for; matrix products, arithmetic and copies ran while one was open for 19% of the time, Pallas kernels for 0%

commit v1 on v0

v1 whole, which is shorter than its diff:
```python
import functools

import jax
import jax.numpy as jnp
from jax import lax
from jax.experimental import pallas as pl
from jax.experimental.pallas import tpu as pltpu
from jax.sharding import PartitionSpec as P

LINE = 4
EXTRA = 16
MIB = 1 << 20
F32 = jnp.float32
BF16 = jnp.bfloat16


def dot(a, b, contract):
    return lax.dot_general(a, b, (contract, ((), ())), preferred_element_type=F32)


def params(limit=48):
    return pltpu.CompilerParams(vmem_limit_bytes=limit * MIB)


def cost(flops, size):
    return pl.CostEstimate(flops=int(flops), bytes_accessed=int(size), transcendentals=0)


def whole():
    return pl.BlockSpec(memory_space=pltpu.VMEM)


def smem():
    return pl.BlockSpec(memory_space=pltpu.SMEM)


def gate_kernel(routes_ref, x_ref, router_ref, out_ref):
    logits = dot(router_ref[...], x_ref[...], ((1,), (1,)))
    row = lax.broadcasted_iota(jnp.int32, logits.shape, 0)
    member = row == routes_ref[0:1, :]
    for k in range(1, routes_ref.shape[0]):
        member = member | (row == routes_ref[k : k + 1, :])
    top = jnp.max(jnp.where(member, logits, -jnp.inf), axis=0, keepdims=True)
    weight = jnp.where(member, jnp.exp(logits - top), 0.0)
    out_ref[...] = jnp.where(member, weight / jnp.sum(weight, axis=0, keepdims=True), -1.0)


def rank_of(prob):
    count = prob.shape[1]
    earlier = lax.broadcasted_iota(jnp.int32, (count, count), 0) < lax.broadcasted_iota(
        jnp.int32, (count, count), 1
    )
    member = prob >= 0.0
    rank = dot(member.astype(F32).astype(BF16), earlier.astype(F32).astype(BF16), ((1,), (0,)))
    return jnp.where(member, rank, -1.0)


def slots(rank_row, count, first):
    row = lax.broadcasted_iota(jnp.int32, (count, rank_row.shape[1]), 0).astype(F32)
    return (row + first == rank_row).astype(F32)


def extra_slots(rank_row, main, r):
    row = lax.broadcasted_iota(jnp.int32, (EXTRA, rank_row.shape[1]), 0).astype(F32) - 2.0 * r
    return ((row >= 0.0) & (row < 2.0) & (row + main == rank_row)).astype(F32)


def compact_kernel(plane, main, scaled, extra, place_ref, *refs):
    blocks = LINE if extra else 1
    z, q, end = place_ref[0], place_ref[1], place_ref[2]
    refs = list(refs)
    prob_refs = [refs.pop(0) for _ in range(blocks)]
    outs = refs[-1 - plane : -1]
    rank_ref = refs[-1]
    cands = refs[: -1 - plane]
    if extra:
        groups = [cands[0:1], cands[1:2], cands[2:4], cands[4:6]]
    else:
        groups = [cands]
    rows = []
    for group in groups:
        block = group[0][...]
        if len(group) == 2:
            block = jnp.where(end > 0, block, group[1][...])
        rows.append(block)

    def gathered(picks, probs, block):
        value = dot(jnp.concatenate(picks, axis=0).astype(BF16), block, ((1,), (0,)))
        if scaled:
            factor = [jnp.sum(a * b, axis=1, keepdims=True) for a, b in zip(picks, probs)]
            value = value * jnp.concatenate(factor, axis=0)
        return value

    tail = None
    for r in range(blocks):
        rank_ref[...] = rank_of(prob_refs[r][...])
        picks, probs, more = [], [], []
        for s in range(plane):
            expert = z * plane + (q ^ s)
            rank_row = rank_ref[pl.ds(expert, 1), :]
            probs.append(prob_refs[r][pl.ds(expert, 1), :])
            picks.append(slots(rank_row, main, 0.0))
            if extra:
                more.append(extra_slots(rank_row, float(main), r))
        if r == blocks - 1:
            value = gathered(picks, probs, rows[r])
            for s in range(plane):
                outs[s][0:main, :] = value[s * main : (s + 1) * main].astype(BF16)
        if extra:
            value = gathered(more, probs, rows[r])
            tail = value if tail is None else tail + value
    if extra:
        for s in range(plane):
            outs[s][main : main + EXTRA, :] = tail[s * EXTRA : (s + 1) * EXTRA].astype(BF16)


def compact(place, probs, cands, plane, main, scaled, extra):
    experts, count = probs[0].shape
    width = cands[0].shape[1]
    height = main + (EXTRA if extra else 0)
    return pl.pallas_call(
        functools.partial(compact_kernel, plane, main, scaled, extra),
        out_shape=[jax.ShapeDtypeStruct((height, width), BF16)] * plane,
        in_specs=[smem()] + [whole()] * (len(probs) + len(cands)),
        out_specs=[whole()] * plane,
        scratch_shapes=[pltpu.VMEM((experts, count), F32)],
        compiler_params=params(),
        cost_estimate=cost(
            2 * plane * height * count * width, 2 * width * (len(cands) * count + plane * height)
        ),
    )(place, *probs, *cands)


def expert_kernel(plane, *refs):
    xs, ss = refs[:plane], refs[plane : 2 * plane]
    gate_ref, up_ref, down_ref = refs[2 * plane : 2 * plane + 3]
    parts = refs[2 * plane + 3 : 3 * plane + 3]
    hidden_ref, gg_ref, gu_ref, rows_x, rows_s, score_ref, total, score = refs[3 * plane + 3 :]
    height = xs[0].shape[0]
    step, last = pl.program_id(0), pl.num_programs(0) - 1

    @pl.when(step == 0)
    def _():
        for s in range(plane):
            rows_x[s * height : (s + 1) * height, :] = xs[s][...]
            rows_s[s * height : (s + 1) * height, :] = ss[s][...]
        total[...] = jnp.zeros_like(total)
        score[...] = jnp.zeros_like(score)

    gate_w, up_w, down_w = gate_ref[0], up_ref[0], down_ref[0]
    pre_gate = dot(rows_x[...], gate_w, ((1,), (1,)))
    pre_up = dot(rows_x[...], up_w, ((1,), (1,)))
    grad_hidden = dot(rows_s[...], down_w, ((1,), (1,)))
    sig = jax.nn.sigmoid(pre_gate)
    act = pre_gate * sig
    hidden = (act * pre_up).astype(BF16)
    grad_pg = (grad_hidden * pre_up * sig * (1.0 + pre_gate * (1.0 - sig))).astype(BF16)
    grad_pu = (grad_hidden * act).astype(BF16)
    hidden_ref[...] = hidden
    gg_ref[...] = grad_pg
    gu_ref[...] = grad_pu
    score[...] += jnp.sum(hidden.astype(F32) * grad_hidden, axis=1, keepdims=True)
    total[...] += dot(grad_pg, gate_w, ((1,), (0,))) + dot(grad_pu, up_w, ((1,), (0,)))

    @pl.when(step == last)
    def _():
        for s in range(plane):
            parts[s][...] = total[s * height : (s + 1) * height, :].astype(BF16)
        spread = jnp.broadcast_to(score[...], (score.shape[0], 128))
        score_ref[...] = spread.T[0:8, :]


def expert(xs, ss, gate_w, up_w, down_w):
    plane = len(xs)
    height, width = xs[0].shape
    rows = plane * height
    hid = gate_w.shape[1]
    tile = 256 if hid % 256 == 0 else hid
    wspec = pl.BlockSpec((1, tile, width), lambda i: (0, i, 0))
    part = pl.BlockSpec((height, width), lambda i: (0, 0))
    narrow = pl.BlockSpec((rows, tile), lambda i: (0, i))
    full = pl.BlockSpec((rows, width), lambda i: (0, 0))
    out = pl.pallas_call(
        functools.partial(expert_kernel, plane),
        grid=(hid // tile,),
        out_shape=[jax.ShapeDtypeStruct((height, width), BF16)] * plane
        + [jax.ShapeDtypeStruct((rows, hid), BF16)] * 3
        + [jax.ShapeDtypeStruct((rows, width), BF16)] * 2
        + [jax.ShapeDtypeStruct((8, rows), F32)],
        in_specs=[part] * (2 * plane) + [wspec] * 3,
        out_specs=[part] * plane
        + [narrow] * 3
        + [full] * 2
        + [pl.BlockSpec((8, rows), lambda i: (0, 0))],
        scratch_shapes=[pltpu.VMEM((rows, width), F32), pltpu.VMEM((rows, 1), F32)],
        compiler_params=params(),
        cost_estimate=cost(10 * rows * width * hid, 6 * hid * width + 10 * rows * width),
    )(*xs, *ss, gate_w, up_w, down_w)
    return out[:plane], out[plane : plane + 3], out[plane + 3 : plane + 5], out[plane + 5]


def weight_kernel(chunks, added, half_ref, *refs):
    xs, ss = refs[:chunks], refs[chunks : 2 * chunks]
    hs, ggs, gus = (refs[(2 + i) * chunks : (3 + i) * chunks] for i in range(3))
    refs = refs[5 * chunks :]
    for i, (left, right) in enumerate(((ggs, xs), (gus, xs), (hs, ss))):
        total = dot(left[0][...], right[0][...], ((0,), (0,)))
        for r in range(1, chunks):
            total = total + dot(left[r][...], right[r][...], ((0,), (0,)))
        if added:
            refs[3 + i][0] = (total + refs[i][...].astype(F32)).astype(BF16)
        else:
            refs[i][...] = total.astype(BF16)


def weight_grads(half, xs, ss, hs, ggs, gus, parts, other):
    chunks = len(xs)
    width = xs[0].shape[1]
    rows = hs[0].shape[1] // parts
    fixed = [pl.BlockSpec(a.shape, lambda i, ref: (0, 0)) for a in (*xs, *ss)]
    cut = [pl.BlockSpec((a.shape[0], rows), lambda i, ref: (0, ref[0])) for a in (*hs, *ggs, *gus)]
    flat = pl.BlockSpec((rows, width), lambda i, ref: (0, 0))
    if other is None:
        out_spec, shape, given = flat, (rows, width), ()
    else:
        out_spec, shape, given = (
            pl.BlockSpec((1, rows, width), lambda i, ref: (0, 0, 0)),
            (1, rows, width),
            tuple(other),
        )
    count = sum(a.shape[0] for a in xs)
    return pl.pallas_call(
        functools.partial(weight_kernel, chunks, other is not None),
        grid_spec=pltpu.PrefetchScalarGridSpec(
            num_scalar_prefetch=1,
            grid=(1,),
            in_specs=fixed + cut + [flat] * len(given),
            out_specs=[out_spec] * 3,
        ),
        out_shape=[jax.ShapeDtypeStruct(shape, BF16)] * 3,
        compiler_params=params(60),
        cost_estimate=cost(6 * count * rows * width, 4 * count * width + 6 * rows * width),
    )(half, *xs, *ss, *hs, *ggs, *gus, *given)


def scatter_kernel(plane, main, r, added, last, place_ref, prob_ref, *refs):
    refs = list(refs)
    rows_ref, more_ref, rank_ref = refs[-3:]
    out_ref = refs[-4]
    backs, refs = refs[:plane], refs[plane:-4]
    tails, refs = refs[:plane], refs[plane:]
    z, q = place_ref[0], place_ref[1]
    rank_ref[...] = rank_of(prob_ref[...])
    picks, more = [], []
    for s in range(plane):
        rank_row = rank_ref[pl.ds(z * plane + (q ^ s), 1), :]
        picks.append(slots(rank_row, main, 0.0))
        more.append(extra_slots(rank_row, float(main), r))
        rows_ref[s * main : (s + 1) * main, :] = backs[s][...]
        more_ref[s * EXTRA : (s + 1) * EXTRA, :] = tails[s][...]
    total = dot(jnp.concatenate(picks, axis=0).astype(BF16), rows_ref[...], ((0,), (0,)))
    total = total + dot(jnp.concatenate(more, axis=0).astype(BF16), more_ref[...], ((0,), (0,)))
    for i in range(added):
        total = total + refs[i][...].astype(F32)
    if last:
        total = total + dot(refs[added][...], refs[added + 1][...], ((0,), (0,)))
    out_ref[...] = total.astype(BF16)


def scatter(place, prob, backs, tails, main, r, added, router=()):
    plane = len(backs)
    width = backs[0].shape[1]
    experts, count = prob.shape
    head = pl.BlockSpec((main, width), lambda i: (0, 0))
    tail = pl.BlockSpec((EXTRA, width), lambda i: (main // EXTRA, 0))
    dense = pl.BlockSpec((count, width), lambda i: (0, 0))
    fixed = lambda a: pl.BlockSpec(a.shape, lambda i: (0, 0))
    return pl.pallas_call(
        functools.partial(scatter_kernel, plane, main, r, len(added), len(router) > 0),
        grid=(1,),
        out_shape=jax.ShapeDtypeStruct((count, width), BF16),
        in_specs=[smem(), fixed(prob)]
        + [head] * plane
        + [tail] * plane
        + [dense] * len(added)
        + [fixed(a) for a in router],
        out_specs=dense,
        scratch_shapes=[
            pltpu.VMEM((plane * main, width), BF16),
            pltpu.VMEM((plane * EXTRA, width), BF16),
            pltpu.VMEM((experts, count), F32),
        ],
        compiler_params=params(),
        cost_estimate=cost(2 * plane * (main + EXTRA) * count * width, 6 * plane * main * width),
    )(place, prob, *backs, *tails, *added, *router)


def router_kernel(prob_ref, score_ref, x_ref, dlogits_ref, term_ref, dense_ref):
    prob = prob_ref[...]
    rank = rank_of(prob)
    member = prob >= 0.0
    score = score_ref[...]
    high = score.astype(BF16)
    rest = score - high.astype(F32)
    mid = rest.astype(BF16)
    low = (rest - mid.astype(F32)).astype(BF16)
    for e in range(prob.shape[0]):
        pick = slots(rank[e : e + 1, :], score.shape[1], 0.0).astype(BF16)
        value = dot(high[e : e + 1, :], pick, ((1,), (0,)))
        value = value + dot(mid[e : e + 1, :], pick, ((1,), (0,)))
        dense_ref[e : e + 1, :] = value + dot(low[e : e + 1, :], pick, ((1,), (0,)))
    weighted = dense_ref[...]
    both = weighted - prob * jnp.sum(weighted, axis=0, keepdims=True)
    dlogits = jnp.where(member, both, 0.0).astype(BF16)
    dlogits_ref[...] = dlogits
    term_ref[...] = dot(dlogits, x_ref[...], ((1,), (0,)))


def router_grads(prob, score, x):
    experts, count = prob.shape
    width = x.shape[1]
    return pl.pallas_call(
        router_kernel,
        out_shape=[
            jax.ShapeDtypeStruct((experts, count), BF16),
            jax.ShapeDtypeStruct((experts, width), F32),
        ],
        in_specs=[whole()] * 3,
        out_specs=[whole()] * 2,
        scratch_shapes=[pltpu.VMEM((experts, count), F32)],
        compiler_params=params(),
        cost_estimate=cost(2 * experts * count * (width + 3 * count), 2 * count * width),
    )(prob, score, x)


def local(tokens_in, grad_out, routes, router_weight, w_gate, w_up, w_down):
    tok_count, width = tokens_in.shape
    top_count = routes.shape[1]
    experts = router_weight.shape[1]
    main = tok_count * top_count // experts
    cap = main + 2
    plane = experts // LINE
    me = lax.axis_index("expert")
    core = lax.axis_index("dp")
    z, q = me // plane, me % plane
    end = ((z == 0) | (z == LINE - 1)).astype(jnp.int32)
    place = jnp.stack([z, q, end]).astype(jnp.int32)
    router_t = router_weight.T

    def line(pairs):
        return [(a * plane + i, b * plane + i) for a, b in pairs for i in range(plane)]

    pair_swap = line([(0, 1), (1, 0), (2, 3), (3, 2)])
    mid_swap = line([(1, 2), (2, 1)])
    outward = line([(1, 0), (2, 3)])
    inward = line([(0, 1), (3, 2)])
    send = lambda a, perm: lax.ppermute(a, "expert", perm)
    across = lambda a, bit: send(a, [(i, i ^ bit) for i in range(experts)])

    prob = pl.pallas_call(
        gate_kernel,
        out_shape=jax.ShapeDtypeStruct((experts, tok_count), F32),
        in_specs=[whole()] * 3,
        out_specs=whole(),
        compiler_params=params(),
        cost_estimate=cost(2 * experts * tok_count * width, 2 * tok_count * width),
    )(routes.T, tokens_in, router_t)
    probs = [prob] + [across(prob, r * plane) for r in range(1, LINE)]

    def along(a):
        near, mid = send(a, pair_swap), send(a, mid_swap)
        near2, mid2 = send(mid, outward), send(near, mid_swap)
        far = send(mid2, outward)
        return [(a,), (near,), (near2, mid2), (far, mid)]

    cand_x, cand_g = along(tokens_in), along(grad_out)

    def spread(cands, r, scaled):
        extra = r == LINE - 1
        if extra:
            given = [c for group in cands for c in group]
            rows = compact(place, probs, given, plane, main, scaled, True)
        else:
            rows = compact(place, probs[r : r + 1], cands[r], plane, main, scaled, False)
        return [rows[0]] + [across(rows[s], s) for s in range(1, plane)]

    parts, narrow, rows, scores = {}, {}, {}, {}
    for r in (0, 1, 3, 2):
        x_rows, s_rows = spread(cand_x, r, False), spread(cand_g, r, True)
        parts[r], narrow[r], rows[r], scores[r] = expert(x_rows, s_rows, w_gate, w_up, w_down)

    heads = [scores[r][0].reshape(plane, -1) for r in range(LINE)]
    tails = heads[-1][:, main : main + 2 * LINE].reshape(plane, LINE, 2).transpose(1, 0, 2)
    heads = jnp.stack([h[:, :main] for h in heads])
    packed = jnp.concatenate([heads, tails], axis=2).reshape(experts, cap)
    packed = jnp.pad(packed, ((0, 0), (0, tok_count - cap)))
    packed = packed[jnp.arange(experts) ^ me]
    score = lax.all_to_all(packed, "expert", split_axis=0, concat_axis=0, tiled=True)
    dlogits, term = router_grads(prob, score, tokens_in)
    for bit in range(experts.bit_length() - 1):
        term = term + across(term, 1 << bit)
    term = term + lax.ppermute(term, "dp", [(0, 1), (1, 0)])
    grad_router = term.T / tok_count

    back = {}
    for r in (3, 2, 1, 0):
        back[r] = [parts[r][0]] + [across(parts[r][s], s) for s in range(1, plane)]
    extra = back[LINE - 1]
    join = lambda r, added, router=(): scatter(
        place, probs[r], back[r], extra, main, r, added, router
    )
    far = join(3, [])
    sum2 = join(2, [send(far, inward)])
    far = (far.astype(F32) + send(sum2, inward).astype(F32)).astype(BF16)
    sum1 = join(1, [send(sum2, mid_swap)])
    grad_x = join(0, [send(sum1, pair_swap), send(far, mid_swap)], (dlogits, router_t))

    order = range(LINE)
    given = (
        [rows[r][0] for r in order],
        [rows[r][1] for r in order],
        [narrow[r][0] for r in order],
        [narrow[r][1] for r in order],
        [narrow[r][2] for r in order],
    )
    replicas = 2
    half = core.reshape(1).astype(jnp.int32)
    gone = weight_grads(1 - half, *given, replicas, None)
    other = [lax.ppermute(a, "dp", [(0, 1), (1, 0)]) for a in gone]
    grad_gate, grad_up, grad_down = weight_grads(half, *given, replicas, other)
    return (grad_x, grad_gate, grad_up, grad_down, grad_router)


def solution(mesh):
    return jax.shard_map(
        local,
        mesh=mesh,
        in_specs=(
            P(("dp", "expert"), None),
            P(("dp", "expert"), None),
            P(("dp", "expert"), None),
            P(),
            P("expert", None, None),
            P("expert", None, None),
            P("expert", None, None),
        ),
        out_specs=(
            P(("dp", "expert"), None),
            P("expert", "dp", None),
            P("expert", "dp", None),
            P("expert", "dp", None),
            P(),
        ),
        check_vma=False,
    )
```

time: 543 us -> 305 us (0.56); the launches traced: 535 us -> 304 us
  waiting for transfers between devices: 267 us -> 67.7 us
  Pallas kernels: 0 us -> 103 us
  local copies, waits for them, and re-layouts: 99.3 us -> 33.1 us
  matrix products: 58.6 us -> 0 us
  other arithmetic: 34.5 us -> 3.45 us
  starting transfers between devices: 59.6 us -> 84.1 us
  between operations: 16.2 us -> 1.21 us
  blocking collectives: 0 us -> 12 us
    all_to_all x4 -> x0, waiting for transfers between devices: 134 us -> none  [the longest x1 69.3 us: local(): lax.all_to_all(sent_s, 'expert', split_axis=0, concat_axis=0, tiled=True)]
    psum x1 -> x0, waiting for transfers between devices: 133 us -> none  [local(): grad_router = lax.psum(router_term, ('dp', 'expert')) / tok_count]
    pallas_call x0 -> x20, Pallas kernels: none -> 103 us  [the longest x4 51.4 us: expert(): pl.pallas_call(functools.partial(expert_kernel, plane), grid=(hid // tile...]
    ppermute x0 -> x62, starting transfers between devices: none -> 84.1 us  [the longest x58 83.4 us: local(): send = lambda a, perm: lax.ppermute(a, 'expert', perm)]
    ppermute x0 -> x62, waiting for transfers between devices: none -> 67.7 us  [the longest x58 67.6 us: local(): send = lambda a, perm: lax.ppermute(a, 'expert', perm)]
    all_to_all x4 -> x0, starting transfers between devices: 59.5 us -> none  [the longest x1 22.6 us: local(): lax.all_to_all(sent_s, 'expert', split_axis=0, concat_axis=0, tiled=True)]
    dot_general x11 -> x0, matrix products: 58.6 us -> none  [the longest x1 10.9 us: local(): jnp.einsum('rd,fd->rf', rows_s, down_w, preferred_element_type=jnp.float32)]
    gather x11 -> x2, local copies, waits for them, and re-layouts: 58 us -> 0.57 us  [local(): packed = packed[jnp.arange(experts) ^ me]]
  transfers between devices with their start and end apart: 6 -> 62, of which waited for: 3 -> 17; matrix products, arithmetic and copies ran while one was open for 19% -> 1% of each run, Pallas kernels for 0% -> 26%
where the time goes in v1:
time: 305 us; the launch traced here: 304 us
  Pallas kernels  103 us (34%)
  starting transfers between devices  84.1 us (28%)
  waiting for transfers between devices  67.7 us (22%)
  local copies, waits for them, and re-layouts  33.1 us (11%)
  blocking collectives  12 us (4%)
  other arithmetic  3.45 us (1%)
    ppermute x58, starting transfers between devices, local(): send = lambda a, perm: lax.ppermute(a, 'expert', perm)  83.4 us
    ppermute x58, waiting for transfers between devices, local(): send = lambda a, perm: lax.ppermute(a, 'expert', perm)  67.6 us
    pallas_call x4, Pallas kernels, expert(): pl.pallas_call(functools.partial(expert_kernel, plane), grid=(hid // tile...  51.4 us
    unnamed x125, local copies, waits for them, and re-layouts  32 us
    pallas_call x2, Pallas kernels, weight_grads(): pl.pallas_call(functools.partial(weight_kernel, chunks, other is not None...  24.8 us
    pallas_call x8, Pallas kernels, compact(): pl.pallas_call(functools.partial(compact_kernel, plane, main, scaled, ext...  16.8 us
    all_to_all x1, blocking collectives, local(): lax.all_to_all(packed, 'expert', split_axis=0, concat_axis=0, tiled=True)  12 us
    pallas_call x4, Pallas kernels, scatter(): pl.pallas_call(functools.partial(scatter_kernel, plane, main, r, len(adde...  6.49 us
  transfers between devices with their start and end apart: 62, of which 17 were waited for; matrix products, arithmetic and copies ran while one was open for 1% of the time, Pallas kernels for 26%

profile of v1, /device:TPU:0, one launch (start us, length us, event | category | flops | bytes accessed | tf_op | source)
XLA Modules:
  0.0 304.2 jit_solution(11070226052405548773)
XLA Ops:
  5.2 3.0 collective-permute-start.3
  11.3 2.5 collective-permute-start.11
  13.9 11.4 %collective-permute-done.11.refs_3_.prob_ref = f32[16,128]{1,0:T(8,128)S(1)} collective-permute-done((f32[16,128]{1,0:T(8,128)S(1)}, f32[16,128]{1,0:T(8,128)S(1)}, u32[]{:S(2)}, u32[]{:S(2)}) %collective-permute-start.11) | collective-permute-done | bytes 8224 | tf_op jit(solution)/shard_map/ppermute | solution.py:357
  26.0 3.0 collective-permute-done.9.refs_1_.refs_0_.prob_ref
  34.1 3.7 %collective-permute-done.5.refs_7_ = bf16[64,2048]{1,0:T(8,128)(2,1)S(1)} collective-permute-done((bf16[64,2048]{1,0:T(8,128)(2,1)S(1)}, bf16[64,2048]{1,0:T(8,128)(2,1)S(1)}, u32[]{:S(2)}, u32[]{:S(2)}) %collective-permute-start.5) | collective-permute-done | bytes 262176 | tf_op jit(solution)/shard_map/ppermute | solution.py:357
  45.8 3.7 %collective-permute-done.2.refs_3_ = bf16[64,2048]{1,0:T(8,128)(2,1)S(1)} collective-permute-done((bf16[64,2048]{1,0:T(8,128)(2,1)S(1)}, bf16[64,2048]{1,0:T(8,128)(2,1)S(1)}, u32[]{:S(2)}, u32[]{:S(2)}) %collective-permute-start.2) | collective-permute-done | bytes 262176 | tf_op jit(solution)/shard_map/ppermute | solution.py:357
  50.9 2.0 collective-permute-start.35
  52.9 2.9 collective-permute-done.34.refs_5_
  61.1 2.5 collective-permute-start.36
  66.8 2.0 shard_map.121
  70.1 2.5 collective-permute-start.32
  72.6 3.4 %collective-permute-done.31.refs_1_ = bf16[64,2048]{1,0:T(8,128)(2,1)S(1)} collective-permute-done((bf16[64,2048]{1,0:T(8,128)(2,1)S(1)}, bf16[64,2048]{1,0:T(8,128)(2,1)S(1)}, u32[]{:S(2)}, u32[]{:S(2)}) %collective-permute-start.31) | collective-permute-done | bytes 262176 | tf_op jit(solution)/shard_map/ppermute | solution.py:357
  77.3 8.3 %collective-permute-done.24.refs_8_ = bf16[128,2048]{1,0:T(8,128)(2,1)S(1)} collective-permute-done((bf16[128,2048]{1,0:T(8,128)(2,1)S(1)}, bf16[128,2048]{1,0:T(8,128)(2,1)S(1)}, u32[]{:S(2)}, u32[]{:S(2)}) %collective-permute-start.24) | collective-permute-done | bytes 524320 | tf_op jit(solution)/shard_map/ppermute | solution.py:357
  87.8 11.8 %shard_map.113 = (bf16[64,2048]{1,0:T(8,128)(2,1)S(1)}, bf16[64,2048]{1,0:T(8,128)(2,1)}, bf16[64,2048]{1,0:T(8,128)(2,1)}, bf16[64,2048]{1,0:T(8,128)(2,1)}, bf...) custom-call(bf16[64,2048]{1,0:T(8,128)(2,1)S(1)} %get-tuple-element., ...), custom_call_target="tpu_custom_call" | custom-call | flops 4026531840 | bytes 14680064 | tf_op jit(solution)/shard_map/pallas_call | solution.py:183
  107.7 3.4 %shard_map.115 = (bf16[80,2048]{1,0:T(8,128)(2,1)S(1)}, bf16[80,2048]{1,0:T(8,128)(2,1)}, bf16[80,2048]{1,0:T(8,128)(2,1)}, bf16[80,2048]{1,0:T(8,128)(2,1)}) custom-call(s32[3]{0:T(128)S(1)} %pad_add_fusion.place_ref, f32[16,128]{1,0:T(8,128)S(1)} %shard_map.110.refs_0_.prob_ref, f32[16,128]{1,0:T(8,128)S(1)} %collective-permute-done.9.refs_1_.refs_0_.prob_ref, ...), custom_call_target="tpu_custom_call" | custom-call | flops 167772160 | bytes 4456448 | tf_op jit(solution)/shard_map/pallas_call | solution.py:121
  117.4 12.4 %shard_map.119 = (bf16[64,2048]{1,0:T(8,128)(2,1)S(1)}, bf16[64,2048]{1,0:T(8,128)(2,1)S(1)}, bf16[64,2048]{1,0:T(8,128)(2,1)S(1)}, bf16[64,2048]{1,0:T(8,128)(2...) custom-call(bf16[64,2048]{1,0:T(8,128)(2,1)S(1)} %copy-done.37, ...), custom_call_target="tpu_custom_call" | custom-call | flops 4026531840 | bytes 14680064 | tf_op jit(solution)/shard_map/pallas_call | solution.py:183
  134.6 3.3 %shard_map.114 = (bf16[80,2048]{1,0:T(8,128)(2,1)S(1)}, bf16[80,2048]{1,0:T(8,128)(2,1)}, bf16[80,2048]{1,0:T(8,128)(2,1)}, bf16[80,2048]{1,0:T(8,128)(2,1)}) custom-call(s32[3]{0:T(128)S(1)} %pad_add_fusion.place_ref, f32[16,128]{1,0:T(8,128)S(1)} %shard_map.110.refs_0_.prob_ref, f32[16,128]{1,0:T(8,128)S(1)} %collective-permute-done.9.refs_1_.refs_0_.prob_ref, ...), custom_call_target="tpu_custom_call" | custom-call | flops 167772160 | bytes 4456448 | tf_op jit(solution)/shard_map/pallas_call | solution.py:121
  145.0 12.4 %shard_map.122 = (bf16[64,2048]{1,0:T(8,128)(2,1)S(1)}, bf16[64,2048]{1,0:T(8,128)(2,1)S(1)}, bf16[64,2048]{1,0:T(8,128)(2,1)S(1)}, bf16[64,2048]{1,0:T(8,128)(2...) custom-call(bf16[64,2048]{1,0:T(8,128)(2,1)S(1)} %copy-done.43, ...), custom_call_target="tpu_custom_call" | custom-call | flops 4026531840 | bytes 14680064 | tf_op jit(solution)/shard_map/pallas_call | solution.py:183
  165.6 14.9 %shard_map.116 = (bf16[80,2048]{1,0:T(8,128)(2,1)S(1)}, bf16[80,2048]{1,0:T(8,128)(2,1)S(1)}, bf16[80,2048]{1,0:T(8,128)(2,1)S(1)}, bf16[80,2048]{1,0:T(8,128)(2...) custom-call(bf16[80,2048]{1,0:T(8,128)(2,1)S(1)} %copy-done.14, ...), custom_call_target="tpu_custom_call" | custom-call | flops 5033164800 | bytes 15990784 | tf_op jit(solution)/shard_map/pallas_call | solution.py:183
  185.3 12.0 %all_to_all.11 = f32[16,1,128]{2,1,0:T(1,128)S(1)} all-to-all(f32[16,1,128]{2,1,0:T(1,128)S(1)} %bitcast.25), channel_id=1, replica_groups=mesh['dp'=2,'expert'=16] {'expert'}, dimensions={0} | all-to-all | bytes 16384 | tf_op jit(solution)/shard_map/all_to_all | solution.py:398
  206.9 5.8 %collective-permute-done.28.refs_1_.refs_5_ = bf16[80,2048]{1,0:T(8,128)(2,1)S(1)} collective-permute-done((bf16[80,2048]{1,0:T(8,128)(2,1)}, bf16[80,2048]{1,0:T(8,128)(2,1)S(1)}, u32[]{:S(2)}, u32[]{:S(2)}) %collective-permute-start.28) | collective-permute-done | bytes 327712 | tf_op jit(solution)/shard_map/ppermute | solution.py:357
  214.7 4.6 %collective-permute-done.30.refs_3_.refs_7_ = bf16[80,2048]{1,0:T(8,128)(2,1)S(1)} collective-permute-done((bf16[80,2048]{1,0:T(8,128)(2,1)S(1)}, bf16[80,2048]{1,0:T(8,128)(2,1)S(1)}, u32[]{:S(2)}, u32[]{:S(2)}) %collective-permute-start.30) | collective-permute-done | bytes 327712 | tf_op jit(solution)/shard_map/ppermute | solution.py:357
  222.6 2.2 collective-permute-done.46.refs_1_
  224.9 2.5 collective-permute-start.49
  227.4 11.7 %shard_map.128 = (bf16[384,2048]{1,0:T(8,128)(2,1)}, bf16[384,2048]{1,0:T(8,128)(2,1)}, bf16[384,2048]{1,0:T(8,128)(2,1)}) custom-call(s32[1]{0:T(128)S(6)} %sub.8.half_ref, bf16[256,2048]{1,0:T(8,128)(2,1)} %copy-done.44, bf16[256,2048]{1,0:T(8,128)(2,1)} %copy-done.45, bf16[256,2048]{1,0:T(8,128)(2,1)} %copy-done.46, ...), custom_call_target="tpu_custom_call" | custom-call | flops 5133828096 | bytes 13631488 | tf_op jit(solution)/shard_map/pallas_call | solution.py:232
  242.5 3.9 %collective-permute-start.52 = (bf16[128,2048]{1,0:T(8,128)(2,1)S(1)}, bf16[128,2048]{1,0:T(8,128)(2,1)S(1)}, u32[]{:S(2)}, u32[]{:S(2)}) collective-permute-start(bf16[128,2048]{1,0:T(8,128)(2,1)S(1)} %shard_map.124), channel_id=1, source_target_pairs={{0,4},{1,5},{2,6},{3,7},{12,8},{13,9},{14,10},{15,11},{16,20},{17,... | collective-permute-start | bytes 1572872 | tf_op jit(solution)/shard_map/ppermute | solution.py:357
  247.2 8.3 %collective-permute-done.39.refs_3_ = bf16[64,2048]{1,0:T(8,128)(2,1)S(1)} collective-permute-done((bf16[64,2048]{1,0:T(8,128)(2,1)S(1)}, bf16[64,2048]{1,0:T(8,128)(2,1)S(1)}, u32[]{:S(2)}, u32[]{:S(2)}) %collective-permute-start.39) | collective-permute-done | bytes 262176 | tf_op jit(solution)/shard_map/ppermute | solution.py:357
  255.9 7.9 %collective-permute-done.60 = f32[16,2048]{1,0:T(8,128)S(1)} collective-permute-done((f32[16,2048]{1,0:T(8,128)S(1)}, f32[16,2048]{1,0:T(8,128)S(1)}, u32[]{:S(2)}, u32[]{:S(2)}) %collective-permute-start.60) | collective-permute-done | bytes 131104 | tf_op jit(solution)/shard_map/ppermute | solution.py:357
  267.6 15.6 %collective-permute-start.51 = (bf16[128,2048]{1,0:T(8,128)(2,1)S(1)}, bf16[128,2048]{1,0:T(8,128)(2,1)S(1)}, u32[]{:S(2)}, u32[]{:S(2)}) collective-permute-start(bf16[128,2048]{1,0:T(8,128)(2,1)S(1)} %shard_map.125), channel_id=1, source_target_pairs={{0,4},{1,5},{2,6},{3,7},{4,0},{5,1},{6,2},{7,3},{8,12},{9,13},{10,... | collective-permute-start | bytes 1572872 | tf_op jit(solution)/shard_map/ppermute | solution.py:357
  286.2 2.3 collective-permute-start.8
  288.6 13.1 %shard_map.129 = (bf16[1,384,2048]{2,1,0:T(8,128)(2,1)}, bf16[1,384,2048]{2,1,0:T(8,128)(2,1)}, bf16[1,384,2048]{2,1,0:T(8,128)(2,1)}) custom-call(s32[1]{0:T(128)} %bitcast.13.half_ref, bf16[256,2048]{1,0:T(8,128)(2,1)} %copy-done.44, bf16[256,2048]{1,0:T(8,128)(2,1)} %copy-done.45, bf16[256,2048]{1,0:T(8,128)(2,1)} %copy-done.46, ...), custom_call_target="tpu_custom_call" | custom-call | flops 5133828096 | bytes 13631488 | tf_op jit(solution)/shard_map/pallas_call | solution.py:232
  301.7 2.5 shard_map.127
  (261 shorter events, 101.6 us)
Async XLA Ops:
  5.2 25.9 %collective-permute-start.3 = (bf16[64,2048]{1,0:T(8,128)(2,1)S(1)}, bf16[64,2048]{1,0:T(8,128)(2,1)S(1)}, u32[]{:S(2)}, u32[]{:S(2)}) collective-permute-start(bf16[64,2048]{1,0:T(8,128)(2,1)S(1)} %get-tuple-element.90), channel_id=1, source_target_pairs={{0,1},{1,0},{2,3},{3,2},{4,5},{5,4},{6,7},{7,6},{8,9},{9,8},{10,11... | collective-permute-start | bytes 786440 | tf_op jit(solution)/shard_map/ppermute | solution.py:357
  8.2 24.4 %collective-permute-start.4 = (bf16[64,2048]{1,0:T(8,128)(2,1)S(1)}, bf16[64,2048]{1,0:T(8,128)(2,1)S(1)}, u32[]{:S(2)}, u32[]{:S(2)}) collective-permute-start(bf16[64,2048]{1,0:T(8,128)(2,1)S(1)} %get-tuple-element.91), channel_id=1, source_target_pairs={{0,2},{1,3},{2,0},{3,1},{4,6},{5,7},{6,4},{7,5},{8,10},{9,11},{10,... | collective-permute-start | bytes 786440 | tf_op jit(solution)/shard_map/ppermute | solution.py:357
  9.7 32.2 %collective-permute-start.20 = (bf16[128,2048]{1,0:T(8,128)(2,1)}, bf16[128,2048]{1,0:T(8,128)(2,1)S(1)}, u32[]{:S(2)}, u32[]{:S(2)}) collective-permute-start(bf16[128,2048]{1,0:T(8,128)(2,1)} %refs_4_.3), channel_id=1, source_target_pairs={{0,4},{1,5},{2,6},{3,7},{4,0},{5,1},{6,2},{7,3},{8,12},{9,13},{10,... | collective-permute-start | bytes 1572872 | tf_op jit(solution)/shard_map/ppermute | solution.py:357
  42.7 20.9 %collective-permute-start.22 = (bf16[128,2048]{1,0:T(8,128)(2,1)S(1)}, bf16[128,2048]{1,0:T(8,128)(2,1)S(1)}, u32[]{:S(2)}, u32[]{:S(2)}) collective-permute-start(bf16[128,2048]{1,0:T(8,128)(2,1)S(1)} %collective-permute-done.21.refs_9_), channel_id=1, source_target_pairs={{4,0},{5,1},{6,2},{7,3},{8,12},{9,13},{10,14},{11,15},{20,16},{21,... | collective-permute-start | bytes 1572872 | tf_op jit(solution)/shard_map/ppermute | solution.py:357
  56.6 20.1 %collective-permute-start.14 = (bf16[128,2048]{1,0:T(8,128)(2,1)S(1)}, bf16[128,2048]{1,0:T(8,128)(2,1)S(1)}, u32[]{:S(2)}, u32[]{:S(2)}) collective-permute-start(bf16[128,2048]{1,0:T(8,128)(2,1)S(1)} %collective-permute-done.13.refs_9_), channel_id=1, source_target_pairs={{4,0},{5,1},{6,2},{7,3},{8,12},{9,13},{10,14},{11,15},{20,16},{21,... | collective-permute-start | bytes 1572872 | tf_op jit(solution)/shard_map/ppermute | solution.py:357
  57.9 27.7 %collective-permute-start.24 = (bf16[128,2048]{1,0:T(8,128)(2,1)S(1)}, bf16[128,2048]{1,0:T(8,128)(2,1)S(1)}, u32[]{:S(2)}, u32[]{:S(2)}) collective-permute-start(bf16[128,2048]{1,0:T(8,128)(2,1)S(1)} %collective-permute-done.23.refs_7_.refs_2_), channel_id=1, source_target_pairs={{4,0},{5,1},{6,2},{7,3},{8,12},{9,13},{10,14},{11,15},{20,16},{21,... | collective-permute-start | bytes 1572872 | tf_op jit(solution)/shard_map/ppermute | solution.py:357
  65.3 50.6 %collective-permute-start.16 = (bf16[128,2048]{1,0:T(8,128)(2,1)S(1)}, bf16[128,2048]{1,0:T(8,128)(2,1)}, u32[]{:S(2)}, u32[]{:S(2)}) collective-permute-start(bf16[128,2048]{1,0:T(8,128)(2,1)S(1)} %collective-permute-done.15.refs_7_.refs_2_), channel_id=1, source_target_pairs={{4,0},{5,1},{6,2},{7,3},{8,12},{9,13},{10,14},{11,15},{20,16},{21,... | collective-permute-start | bytes 1572872 | tf_op jit(solution)/shard_map/ppermute | solution.py:357
  70.1 41.7 %collective-permute-start.32 = (bf16[64,2048]{1,0:T(8,128)(2,1)}, bf16[64,2048]{1,0:T(8,128)(2,1)}, u32[]{:S(2)}, u32[]{:S(2)}) collective-permute-start(bf16[64,2048]{1,0:T(8,128)(2,1)} %get-tuple-element.111), channel_id=1, source_target_pairs={{0,2},{1,3},{2,0},{3,1},{4,6},{5,7},{6,4},{7,5},{8,10},{9,11},{10,... | collective-permute-start | bytes 786440 | tf_op jit(solution)/shard_map/ppermute | solution.py:357
  76.7 35.7 %collective-permute-start.33 = (bf16[64,2048]{1,0:T(8,128)(2,1)}, bf16[64,2048]{1,0:T(8,128)(2,1)}, u32[]{:S(2)}, u32[]{:S(2)}) collective-permute-start(bf16[64,2048]{1,0:T(8,128)(2,1)} %get-tuple-element.112), channel_id=1, source_target_pairs={{0,3},{1,2},{2,1},{3,0},{4,7},{5,6},{6,5},{7,4},{8,11},{9,10},{10,... | collective-permute-start | bytes 786440 | tf_op jit(solution)/shard_map/ppermute | solution.py:357
  76.7 37.2 %collective-permute-start.43 = (bf16[64,2048]{1,0:T(8,128)(2,1)}, bf16[64,2048]{1,0:T(8,128)(2,1)}, u32[]{:S(2)}, u32[]{:S(2)}) collective-permute-start(bf16[64,2048]{1,0:T(8,128)(2,1)} %get-tuple-element.126), channel_id=1, source_target_pairs={{0,1},{1,0},{2,3},{3,2},{4,5},{5,4},{6,7},{7,6},{8,9},{9,8},{10,11... | collective-permute-start | bytes 786440 | tf_op jit(solution)/shard_map/ppermute | solution.py:357
  86.4 29.0 %collective-permute-start.44 = (bf16[64,2048]{1,0:T(8,128)(2,1)}, bf16[64,2048]{1,0:T(8,128)(2,1)}, u32[]{:S(2)}, u32[]{:S(2)}) collective-permute-start(bf16[64,2048]{1,0:T(8,128)(2,1)} %get-tuple-element.127), channel_id=1, source_target_pairs={{0,2},{1,3},{2,0},{3,1},{4,6},{5,7},{6,4},{7,5},{8,10},{9,11},{10,... | collective-permute-start | bytes 786440 | tf_op jit(solution)/shard_map/ppermute | solution.py:357
  111.8 26.8 %collective-permute-start.45 = (bf16[64,2048]{1,0:T(8,128)(2,1)}, bf16[64,2048]{1,0:T(8,128)(2,1)}, u32[]{:S(2)}, u32[]{:S(2)}) collective-permute-start(bf16[64,2048]{1,0:T(8,128)(2,1)} %get-tuple-element.128), channel_id=1, source_target_pairs={{0,3},{1,2},{2,1},{3,0},{4,7},{5,6},{6,5},{7,4},{8,11},{9,10},{10,... | collective-permute-start | bytes 786440 | tf_op jit(solution)/shard_map/ppermute | solution.py:357
  112.4 27.8 %collective-permute-start.40 = (bf16[64,2048]{1,0:T(8,128)(2,1)}, bf16[64,2048]{1,0:T(8,128)(2,1)}, u32[]{:S(2)}, u32[]{:S(2)}) collective-permute-start(bf16[64,2048]{1,0:T(8,128)(2,1)} %get-tuple-element.122), channel_id=1, source_target_pairs={{0,1},{1,0},{2,3},{3,2},{4,5},{5,4},{6,7},{7,6},{8,9},{9,8},{10,11... | collective-permute-start | bytes 786440 | tf_op jit(solution)/shard_map/ppermute | solution.py:357
  113.9 26.9 %collective-permute-start.41 = (bf16[64,2048]{1,0:T(8,128)(2,1)}, bf16[64,2048]{1,0:T(8,128)(2,1)}, u32[]{:S(2)}, u32[]{:S(2)}) collective-permute-start(bf16[64,2048]{1,0:T(8,128)(2,1)} %get-tuple-element.123), channel_id=1, source_target_pairs={{0,2},{1,3},{2,0},{3,1},{4,6},{5,7},{6,4},{7,5},{8,10},{9,11},{10,... | collective-permute-start | bytes 786440 | tf_op jit(solution)/shard_map/ppermute | solution.py:357
  115.3 26.8 %collective-permute-start.42 = (bf16[64,2048]{1,0:T(8,128)(2,1)}, bf16[64,2048]{1,0:T(8,128)(2,1)}, u32[]{:S(2)}, u32[]{:S(2)}) collective-permute-start(bf16[64,2048]{1,0:T(8,128)(2,1)} %get-tuple-element.124), channel_id=1, source_target_pairs={{0,3},{1,2},{2,1},{3,0},{4,7},{5,6},{6,5},{7,4},{8,11},{9,10},{10,... | collective-permute-start | bytes 786440 | tf_op jit(solution)/shard_map/ppermute | solution.py:357
  115.9 27.8 %collective-permute-start.25 = (bf16[80,2048]{1,0:T(8,128)(2,1)}, bf16[80,2048]{1,0:T(8,128)(2,1)S(1)}, u32[]{:S(2)}, u32[]{:S(2)}) collective-permute-start(bf16[80,2048]{1,0:T(8,128)(2,1)} %get-tuple-element.102), channel_id=1, source_target_pairs={{0,1},{1,0},{2,3},{3,2},{4,5},{5,4},{6,7},{7,6},{8,9},{9,8},{10,11... | collective-permute-start | bytes 983048 | tf_op jit(solution)/shard_map/ppermute | solution.py:357
  138.7 23.5 %collective-permute-start.26 = (bf16[80,2048]{1,0:T(8,128)(2,1)}, bf16[80,2048]{1,0:T(8,128)(2,1)S(1)}, u32[]{:S(2)}, u32[]{:S(2)}) collective-permute-start(bf16[80,2048]{1,0:T(8,128)(2,1)} %get-tuple-element.103), channel_id=1, source_target_pairs={{0,2},{1,3},{2,0},{3,1},{4,6},{5,7},{6,4},{7,5},{8,10},{9,11},{10,... | collective-permute-start | bytes 983048 | tf_op jit(solution)/shard_map/ppermute | solution.py:357
  140.2 22.0 %collective-permute-start.27 = (bf16[80,2048]{1,0:T(8,128)(2,1)}, bf16[80,2048]{1,0:T(8,128)(2,1)S(1)}, u32[]{:S(2)}, u32[]{:S(2)}) collective-permute-start(bf16[80,2048]{1,0:T(8,128)(2,1)} %get-tuple-element.104), channel_id=1, source_target_pairs={{0,3},{1,2},{2,1},{3,0},{4,7},{5,6},{6,5},{7,4},{8,11},{9,10},{10,... | collective-permute-start | bytes 983048 | tf_op jit(solution)/shard_map/ppermute | solution.py:357
  140.7 22.2 %collective-permute-start.17 = (bf16[80,2048]{1,0:T(8,128)(2,1)}, bf16[80,2048]{1,0:T(8,128)(2,1)S(1)}, u32[]{:S(2)}, u32[]{:S(2)}) collective-permute-start(bf16[80,2048]{1,0:T(8,128)(2,1)} %get-tuple-element.98), channel_id=1, source_target_pairs={{0,1},{1,0},{2,3},{3,2},{4,5},{5,4},{6,7},{7,6},{8,9},{9,8},{10,11... | collective-permute-start | bytes 983048 | tf_op jit(solution)/shard_map/ppermute | solution.py:357
  142.2 21.5 %collective-permute-start.18 = (bf16[80,2048]{1,0:T(8,128)(2,1)}, bf16[80,2048]{1,0:T(8,128)(2,1)}, u32[]{:S(2)}, u32[]{:S(2)}) collective-permute-start(bf16[80,2048]{1,0:T(8,128)(2,1)} %get-tuple-element.99), channel_id=1, source_target_pairs={{0,2},{1,3},{2,0},{3,1},{4,6},{5,7},{6,4},{7,5},{8,10},{9,11},{10,... | collective-permute-start | bytes 983048 | tf_op jit(solution)/shard_map/ppermute | solution.py:357
  144.4 19.3 %collective-permute-start.19 = (bf16[80,2048]{1,0:T(8,128)(2,1)}, bf16[80,2048]{1,0:T(8,128)(2,1)}, u32[]{:S(2)}, u32[]{:S(2)}) collective-permute-start(bf16[80,2048]{1,0:T(8,128)(2,1)} %get-tuple-element.100), channel_id=1, source_target_pairs={{0,3},{1,2},{2,1},{3,0},{4,7},{5,6},{6,5},{7,4},{8,11},{9,10},{10,... | collective-permute-start | bytes 983048 | tf_op jit(solution)/shard_map/ppermute | solution.py:357
  203.3 18.8 %collective-permute-start.37 = (bf16[64,2048]{1,0:T(8,128)(2,1)}, bf16[64,2048]{1,0:T(8,128)(2,1)S(1)}, u32[]{:S(2)}, u32[]{:S(2)}) collective-permute-start(bf16[64,2048]{1,0:T(8,128)(2,1)} %copy-done.24), channel_id=1, source_target_pairs={{0,1},{1,0},{2,3},{3,2},{4,5},{5,4},{6,7},{7,6},{8,9},{9,8},{10,11... | collective-permute-start | bytes 786440 | tf_op jit(solution)/shard_map/ppermute | solution.py:357
  205.6 19.2 %collective-permute-start.46 = (bf16[64,2048]{1,0:T(8,128)(2,1)}, bf16[64,2048]{1,0:T(8,128)(2,1)S(1)}, u32[]{:S(2)}, u32[]{:S(2)}) collective-permute-start(bf16[64,2048]{1,0:T(8,128)(2,1)} %copy-done.35), channel_id=1, source_target_pairs={{0,1},{1,0},{2,3},{3,2},{4,5},{5,4},{6,7},{7,6},{8,9},{9,8},{10,11... | collective-permute-start | bytes 786440 | tf_op jit(solution)/shard_map/ppermute | solution.py:357
  212.7 29.9 %collective-permute-start.38 = (bf16[64,2048]{1,0:T(8,128)(2,1)}, bf16[64,2048]{1,0:T(8,128)(2,1)S(1)}, u32[]{:S(2)}, u32[]{:S(2)}) collective-permute-start(bf16[64,2048]{1,0:T(8,128)(2,1)} %copy-done.23), channel_id=1, source_target_pairs={{0,2},{1,3},{2,0},{3,1},{4,6},{5,7},{6,4},{7,5},{8,10},{9,11},{10,... | collective-permute-start | bytes 786440 | tf_op jit(solution)/shard_map/ppermute | solution.py:357
  213.2 25.8 %collective-permute-start.47 = (bf16[64,2048]{1,0:T(8,128)(2,1)}, bf16[64,2048]{1,0:T(8,128)(2,1)}, u32[]{:S(2)}, u32[]{:S(2)}) collective-permute-start(bf16[64,2048]{1,0:T(8,128)(2,1)} %copy-done.32), channel_id=1, source_target_pairs={{0,2},{1,3},{2,0},{3,1},{4,6},{5,7},{6,4},{7,5},{8,10},{9,11},{10,... | collective-permute-start | bytes 786440 | tf_op jit(solution)/shard_map/ppermute | solution.py:357
  219.3 19.8 %collective-permute-start.48 = (bf16[64,2048]{1,0:T(8,128)(2,1)}, bf16[64,2048]{1,0:T(8,128)(2,1)}, u32[]{:S(2)}, u32[]{:S(2)}) collective-permute-start(bf16[64,2048]{1,0:T(8,128)(2,1)} %copy-done.31), channel_id=1, source_target_pairs={{0,3},{1,2},{2,1},{3,0},{4,7},{5,6},{6,5},{7,4},{8,11},{9,10},{10,... | collective-permute-start | bytes 786440 | tf_op jit(solution)/shard_map/ppermute | solution.py:357
  239.1 44.8 %collective-permute-start.54 = (bf16[384,2048]{1,0:T(8,128)(2,1)}, bf16[384,2048]{1,0:T(8,128)(2,1)S(1)}, u32[]{:S(2)}, u32[]{:S(2)}) collective-permute-start(bf16[384,2048]{1,0:T(8,128)(2,1)} %get-tuple-element.158), channel_id=1, source_target_pairs={{0,16},{16,0},{1,17},{17,1},{2,18},{18,2},{3,19},{19,3},{4,20},{20... | collective-permute-start | bytes 4718600 | tf_op jit(solution)/shard_map/ppermute | solution.py:429
  239.2 45.3 %collective-permute-start.55 = (bf16[384,2048]{1,0:T(8,128)(2,1)}, bf16[384,2048]{1,0:T(8,128)(2,1)S(1)}, u32[]{:S(2)}, u32[]{:S(2)}) collective-permute-start(bf16[384,2048]{1,0:T(8,128)(2,1)} %get-tuple-element.159), channel_id=1, source_target_pairs={{0,16},{16,0},{1,17},{17,1},{2,18},{18,2},{3,19},{19,3},{4,20},{20... | collective-permute-start | bytes 4718600 | tf_op jit(solution)/shard_map/ppermute | solution.py:429
  239.6 45.4 %collective-permute-start.56 = (bf16[384,2048]{1,0:T(8,128)(2,1)}, bf16[384,2048]{1,0:T(8,128)(2,1)S(1)}, u32[]{:S(2)}, u32[]{:S(2)}) collective-permute-start(bf16[384,2048]{1,0:T(8,128)(2,1)} %get-tuple-element.160), channel_id=1, source_target_pairs={{0,16},{16,0},{1,17},{17,1},{2,18},{18,2},{3,19},{19,3},{4,20},{20... | collective-permute-start | bytes 4718600 | tf_op jit(solution)/shard_map/ppermute | solution.py:429
  242.5 22.0 %collective-permute-start.52 = (bf16[128,2048]{1,0:T(8,128)(2,1)S(1)}, bf16[128,2048]{1,0:T(8,128)(2,1)S(1)}, u32[]{:S(2)}, u32[]{:S(2)}) collective-permute-start(bf16[128,2048]{1,0:T(8,128)(2,1)S(1)} %shard_map.124), channel_id=1, source_target_pairs={{0,4},{1,5},{2,6},{3,7},{12,8},{13,9},{14,10},{15,11},{16,20},{17,... | collective-permute-start | bytes 1572872 | tf_op jit(solution)/shard_map/ppermute | solution.py:357
  265.5 36.2 %collective-permute-start.53 = (bf16[128,2048]{1,0:T(8,128)(2,1)}, bf16[128,2048]{1,0:T(8,128)(2,1)S(1)}, u32[]{:S(2)}, u32[]{:S(2)}) collective-permute-start(bf16[128,2048]{1,0:T(8,128)(2,1)} %add_convert_fusion), channel_id=1, source_target_pairs={{4,8},{5,9},{6,10},{7,11},{8,4},{9,5},{10,6},{11,7},{20,24},{21,25... | collective-permute-start | bytes 1572872 | tf_op jit(solution)/shard_map/ppermute | solution.py:357
  267.6 34.1 %collective-permute-start.51 = (bf16[128,2048]{1,0:T(8,128)(2,1)S(1)}, bf16[128,2048]{1,0:T(8,128)(2,1)S(1)}, u32[]{:S(2)}, u32[]{:S(2)}) collective-permute-start(bf16[128,2048]{1,0:T(8,128)(2,1)S(1)} %shard_map.125), channel_id=1, source_target_pairs={{0,4},{1,5},{2,6},{3,7},{4,0},{5,1},{6,2},{7,3},{8,12},{9,13},{10,... | collective-permute-start | bytes 1572872 | tf_op jit(solution)/shard_map/ppermute | solution.py:357
  (92 other events, 687.5 us)
